TPU v7x, 256 devices: a whole 4x4x8 slice. The times are simulated.
256 devices in a mesh: row: 8 (over z_lo, x), col: 32 (over y, z_hi, core).
Axes of the slice: x: 4, y: 4, z: 8 (z_hi: 4, z_lo: 2; z = z_hi * 2 + z_lo), core: 2. Of those that a mesh axis runs over, the one named last changes fastest.
Arguments:
- adjoint_field: float32 [3, 256, 256, 256], P(None, 'col', 'row'), may hold values from -6 to 6
- velocity: float32 [3, 256, 256, 256], P(None, 'col', 'row'), may hold values from -6 to 6
- saved_field: bfloat16 [2, 3, 256, 256, 256], P(None, None, 'col', 'row'), may hold values from -6 to 6
- gradient_in: float32 [3, 256, 256, 256], P(None, 'col', 'row'), may hold values from -6 to 6
Outputs:
- adjoint_out: float32 [3, 256, 256, 256], P(None, 'col', 'row')
- velocity_gradient: float32 [3, 256, 256, 256], P(None, 'col', 'row')
All inputs are finite; a program needn't handle non-finite values.
Results may differ from a plain program's by a relative error of at most 0.0011.
Values sent between devices are 32-bit elements; how exact they have to be, the bound alone decides.
A program may use at most 128 MiB of HBM per device.

v0:
```python
import functools
import math

import jax
import jax.numpy as jnp
import numpy as np
from jax import lax
from jax.experimental import pallas as pl
from jax.experimental.pallas import tpu as pltpu
from jax.sharding import PartitionSpec as P

TIME_STEP = 0.1
DIFFUSIVITY = 0.5
MESH = pl.DeviceIdType.MESH
LANES = 128
HALVES = 2


def line_tables(length):
    index = np.arange(length)
    signed = np.where(index < length // 2, index, index - length).astype(np.float64)
    laplace = 2.0 * math.pi / length * signed
    laplace[length // 2] = 0.0
    angle = 2.0 * math.pi / length * (index[:, None] * index[None, :] % length)
    wave = np.exp(1j * angle) / math.sqrt(length)
    first = ((wave * (1j * laplace)) @ wave.conj().T).real
    second = ((wave * (-(laplace**2))) @ wave.conj().T).real
    return first, second


def split_parts(values):
    high = values.astype(jnp.bfloat16)
    low = (values - high.astype(jnp.float32)).astype(jnp.bfloat16)
    return high, low


def wait_bytes(ref, sem):
    pltpu.make_async_copy(ref, ref, sem).wait()


def kernel(
    rows, cols,
    a0_in, vel_in, saved_in, grad_in, left_p_in, left_q_in, right_in,
    out_there, vgrad_there,
    out, vgrad, out_sem, a0, vel, saved, grad, left_p_f32, left_q_f32, right_f32, load_sem, left_p, left_q, right,
    a1, mate, curl0, line_r, qbuf, pbuf, qres, pres, qback, pback, send_sem, recv_sem, mate_send, mate_recv,
):
    row, col = lax.axis_index("row"), lax.axis_index("col")
    n_p, n_q, length = a0.shape[1], a0.shape[2], a0.shape[3]
    half_q = length // 2
    block_p = length // 4

    zl, x = lax.div(row, 4), lax.rem(row, 4)
    zh, spot = lax.rem(lax.div(col, 2), 4), lax.div(col, 8) * 2 + lax.rem(col, 2)
    mate_row = lax.rem(row + 4, rows)
    near = lax.rem(zh + 3 + 2 * zl, 4)
    above, below = lax.rem(zh + 1, 4), lax.rem(zh + 3, 4)

    def col_of(spot_there, zh_there):
        return lax.div(spot_there, 2) * 8 + zh_there * 2 + lax.rem(spot_there, 2)

    def spot_at(j):
        return lax.rem(spot + j, 8)

    loads = (
        (left_p_in, left_p_f32), (left_q_in, left_q_f32), (right_in, right_f32),
        (vel_in, vel), (grad_in, grad), (saved_in, saved),
    )
    for half in range(HALVES):
        for member in range(3):
            part = (member, slice(None), slice(None), pl.ds(half * LANES, LANES))
            pltpu.make_async_copy(a0_in.at[part], a0.at[part], load_sem.at[half]).start()
    for at, (there, held) in enumerate(loads):
        pltpu.make_async_copy(there, held, load_sem.at[HALVES + at]).start()

    def loaded(first, last):
        for at in range(first, last):
            there, held = loads[at]
            pltpu.make_async_copy(there, held, load_sem.at[HALVES + at]).wait()

    barrier = pltpu.get_barrier_semaphore()

    def greet(row_there, col_there):
        pl.semaphore_signal(barrier, inc=1, device_id=(row_there, col_there), device_id_type=MESH)

    def greet_spots(j, carry):
        there = spot_at(j)
        greet(row, col_of(there, above))
        greet(row, col_of(there, below))
        greet(mate_row, col_of(there, near))
        return carry

    def greet_zh(j, carry):
        greet(row, col_of(spot_at(j), zh))
        return carry

    def greet_x(j, carry):
        greet(zl * 4 + lax.rem(x + j, 4), col)
        return carry

    greet(mate_row, col)
    lax.fori_loop(0, 8, greet_spots, 0)
    lax.fori_loop(1, 8, greet_zh, 0)
    lax.fori_loop(1, 4, greet_x, 0)
    pl.semaphore_wait(barrier, 1 + 24 + 7 + 3)

    def remote(src, dst, kind, sec, half, row_there, col_there):
        pltpu.make_async_remote_copy(
            src_ref=src, dst_ref=dst, send_sem=send_sem.at[kind, sec, half], recv_sem=recv_sem.at[kind, sec, half],
            device_id=(row_there, col_there), device_id_type=MESH,
        ).start()

    def here(src, dst, kind, sec, half):
        pltpu.make_async_copy(src, dst, recv_sem.at[kind, sec, half]).start()

    def p_line(field, sec, half, row_there, spot_there, zh_there, role):
        lanes = pl.ds(half * LANES, LANES)
        line = col_of(spot_there, lax.rem(zh_there + 4 - role, 4))
        return (
            field.at[:, :, line, lanes],
            pbuf.at[sec, half, role, :, lax.div(col, 8), zh, pl.ds(pl.multiple_of(lax.rem(col, 2) * n_p, n_p), n_p), :],
        )

    def send_line(field, sec, half, row_there, spot_there, zh_there, role, kind, arrival):
        src, dst = p_line(field, sec, half, row_there, spot_there, zh_there, role)
        pltpu.make_async_remote_copy(
            src_ref=src, dst_ref=dst, send_sem=send_sem.at[kind, sec, half], recv_sem=recv_sem.at[arrival, sec, half],
            device_id=(row_there, col_of(spot_there, zh_there)), device_id_type=MESH,
        ).start()

    near_arrival = (1 + 3 * zl, 5 - 4 * zl)

    def pass_on(sec, half):
        for role, source, there in ((0, below, above), (1, above, below)):
            lines = pbuf.at[sec, half, role, :, :, source]
            wait_bytes(lines, recv_sem.at[4 + role, sec, half])
            pltpu.make_async_remote_copy(
                src_ref=lines, dst_ref=pbuf.at[sec, half, 1 - role, :, :, source],
                send_sem=send_sem.at[5, sec, half], recv_sem=recv_sem.at[1, sec, half],
                device_id=(row, col_of(spot, there)), device_id_type=MESH,
            ).start()

    def q_lines(field, half, sec, x_there, from_row):
        planes = pl.ds(x_there * 2, 2)
        return (
            field.at[:, planes, :, pl.ds(half * LANES, LANES)],
            qbuf.at[sec, half, :, :, pl.ds(pl.multiple_of(from_row * n_q, n_q), n_q), :],
        )

    def send_q(field, sec, half, from_row):
        def to_x(j, carry):
            x_there = lax.rem(x + j, 4)
            src, dst = q_lines(field, half, sec, x_there, from_row)
            remote(src, dst, 0, sec, half, zl * 4 + x_there, col)
            return carry

        lax.fori_loop(1, 4, to_x, 0)
        src, dst = q_lines(field, half, sec, x, from_row)
        here(src, dst, 0, sec, half)

    def mate_part(c):
        y_there = lax.rem(lax.div(spot, 2) + c, 4)
        return y_there, pl.ds(pl.multiple_of(y_there * 8, 8), 8)

    def start_mate(field, sec, half, c):
        lanes = pl.ds(half * LANES, LANES)
        _, part = mate_part(c)
        pltpu.make_async_remote_copy(
            src_ref=field.at[:, :, part, lanes], dst_ref=mate.at[sec, :, :, part, lanes],
            send_sem=mate_send.at[sec, half], recv_sem=mate_recv.at[sec, half, c],
            device_id=(mate_row, col), device_id_type=MESH,
        ).start()

    def pass_mate(sec, half, c):
        y_there, part = mate_part(c)
        wait_bytes(mate.at[sec, :, :, part, pl.ds(half * LANES, LANES)], mate_recv.at[sec, half, c])
        for core in range(2):
            there = y_there * 2 + core
            for role in range(2):
                send_line(mate.at[sec], sec, half, mate_row, there, near, role, 4, near_arrival[role])

    def send_near(field, sec, half, c):
        y_there, _ = mate_part(c)
        for core in range(2):
            for role in range(2):
                send_line(field, sec, half, row, y_there * 2 + core, near, role, 4, near_arrival[role])

    def send_zh(field, sec, half):
        def to_spot(j, carry):
            for role in range(2):
                send_line(field, sec, half, row, spot_at(j), zh, role, 1, 1)
            return carry

        lax.fori_loop(1, 8, to_spot, 0)
        for role in range(2):
            src, dst = p_line(field, sec, half, row, spot, zh, role)
            here(src, dst, 1, sec, half)

    def parts(step):
        def body(c, carry):
            step(c)
            return carry

        lax.fori_loop(0, 4, body, 0)

    def first_sends(field, sec):
        parts(lambda c: (start_mate(field, sec, 0, c), send_near(field, sec, 0, c)))
        send_zh(field, sec, 0)
        send_q(field, sec, 0, row)

    def other_sends(field, sec):
        parts(lambda c: (pass_mate(sec, 0, c), start_mate(field, sec, 1, c)))
        parts(lambda c: send_near(field, sec, 1, c))
        send_zh(field, sec, 1)
        send_q(field, sec, 1, row)
        send_q(mate.at[sec], sec, 0, mate_row)
        parts(lambda c: pass_mate(sec, 1, c))
        pass_on(sec, 0)
        send_q(mate.at[sec], sec, 1, mate_row)
        pass_on(sec, 1)

    def line_ops(sec):
        for half in range(HALVES):
            p_ops(sec, half)
            q_ops(sec, half)

    def stack(lines):
        high, low = split_parts(lines)
        return jnp.concatenate([high, low, high], axis=0)

    def whole(lines):
        return lines.reshape(length, LANES)

    def p_ops(sec, half):
        wait_bytes(pbuf.at[sec, half, :, :, pl.ds(0, 3)], recv_sem.at[1, sec, half])
        for role, beside in ((0, below), (1, above)):
            lines = jnp.concatenate([whole(pbuf[sec, half, role, 1]), whole(pbuf[sec, half, role, 2])], axis=1)
            table = jnp.concatenate([left_p[zh], left_p[beside]], axis=0)
            both = jnp.dot(table, stack(lines), preferred_element_type=jnp.float32)
            table = jnp.concatenate([left_p[zh, block_p:], left_p[beside, block_p:]], axis=0)
            second = jnp.dot(table, stack(whole(pbuf[sec, half, role, 0])), preferred_element_type=jnp.float32)
            for at in range(2):
                base = at * 2 * block_p
                for member in range(2):
                    lanes = slice(member * LANES, (member + 1) * LANES)
                    pres[sec, half, role, member, at] = both[base : base + block_p, lanes]
                    pres[sec, half, role, 3 + member, at] = both[base + block_p : base + 2 * block_p, lanes]
                pres[sec, half, role, 2, at] = second[at * block_p : (at + 1) * block_p]

        def result(role, at, there):
            line = col_of(spot, lax.rem(zh + 4 - role, 4))
            return (
                pres.at[sec, half, role, :, at, pl.ds(pl.multiple_of(there * n_p, n_p), n_p), :],
                pback.at[sec, half, :, :, line, :],
            )

        def to_spot(j, carry):
            there = spot_at(j)
            for role, beside in ((0, below), (1, above)):
                src, dst = result(role, 1, there)
                remote(src, dst, 3, sec, half, row, col_of(there, beside))
            return carry

        def to_zh(j, carry):
            there = spot_at(j)
            for role in range(2):
                src, dst = result(role, 0, there)
                remote(src, dst, 3, sec, half, row, col_of(there, zh))
            return carry

        lax.fori_loop(0, 8, to_spot, 0)
        lax.fori_loop(1, 8, to_zh, 0)
        for role in range(2):
            src, dst = result(role, 0, spot)
            here(src, dst, 3, sec, half)

    def q_ops(sec, half):
        wait_bytes(qbuf.at[sec, half], recv_sem.at[0, sec, half])
        for member in range(3):
            lines = stack(jnp.concatenate([qbuf[sec, half, member, 0], qbuf[sec, half, member, 1]], axis=1))
            if member == 1:
                second = jnp.dot(left_q[zl, half_q:], lines, preferred_element_type=jnp.float32)
            else:
                both = jnp.dot(left_q[zl], lines, preferred_element_type=jnp.float32)
                second = both[half_q:]
            for plane in range(2):
                lanes = slice(plane * LANES, (plane + 1) * LANES)
                if member != 1:
                    qres[sec, half, member // 2, plane] = both[:half_q, lanes]
                qres[sec, half, 2 + member, plane] = second[:, lanes]

        def result(x_there):
            return (
                qres.at[sec, half, :, :, pl.ds(pl.multiple_of(x_there * n_q, n_q), n_q), :],
                qback.at[sec, half, :, pl.ds(x * 2, 2)],
            )

        def to_x(j, carry):
            x_there = lax.rem(x + j, 4)
            src, dst = result(x_there)
            remote(src, dst, 2, sec, half, zl * 4 + x_there, col)
            return carry

        lax.fori_loop(1, 4, to_x, 0)
        src, dst = result(x)
        here(src, dst, 2, sec, half)

    def wait_back(sec, half):
        wait_bytes(qback.at[sec, half], recv_sem.at[2, sec, half])
        wait_bytes(pback.at[sec, half], recv_sem.at[3, sec, half])

    def along_r(field):
        def plane(p, carry):
            for member in range(3):
                high, low = split_parts(field[member, p])
                stacked = jnp.concatenate([high, low, high], axis=1)
                if member < 2:
                    both = jnp.dot(stacked, right[...], preferred_element_type=jnp.float32)
                    line_r[member, p] = both[:, :length]
                    line_r[2 + member, p] = both[:, length:]
                else:
                    line_r[4, p] = jnp.dot(stacked, right[:, length:], preferred_element_type=jnp.float32)
            return carry

        lax.fori_loop(0, n_p, plane, 0)

    def curl_at(sec, half, p, lanes):
        dq0, dq2 = qback[sec, half, 0, p], qback[sec, half, 1, p]
        dp1, dp2 = pback[sec, half, 0, p], pback[sec, half, 1, p]
        dr0, dr1 = line_r[0, p, :, lanes], line_r[1, p, :, lanes]
        return dq2 - dr1, dr0 - dp2, dp1 - dq0

    def laplace_at(sec, half, p, lanes, member):
        return line_r[2 + member, p, :, lanes] + qback[sec, half, 2 + member, p] + pback[sec, half, 2 + member, p]

    def cross(f, g):
        return (f[1] * g[2] - f[2] * g[1], f[2] * g[0] - f[0] * g[2], f[0] * g[1] - f[1] * g[0])

    def first_gradient(p, carry):
        low = [curl0[member, p].astype(jnp.float32) for member in range(3)]
        terms = cross([saved[0, member, p].astype(jnp.float32) for member in range(3)], low)
        for member in range(3):
            vgrad[member, p] = grad[member, p] + 0.5 * TIME_STEP * terms[member]
        return carry

    for half in range(HALVES):
        wait_bytes(a0.at[:, :, :, pl.ds(half * LANES, LANES)], load_sem.at[half])
    first_sends(a0, 0)
    loaded(0, 3)
    for table, held, axis in ((left_p_f32, left_p, 2), (left_q_f32, left_q, 2), (right_f32, right, 0)):
        high, low = split_parts(table[...])
        held[...] = jnp.concatenate([high, high, low], axis=axis)
    other_sends(a0, 0)
    line_ops(0)
    along_r(a0)
    loaded(3, 6)

    for half in range(HALVES):
        lanes = pl.ds(half * LANES, LANES)
        wait_back(0, half)

        def first_step(p, carry):
            curl = curl_at(0, half, p, lanes)
            rate = cross(curl, [vel[member, p, :, lanes] for member in range(3)])
            for member in range(3):
                curl0[member, p, :, lanes] = curl[member].astype(jnp.bfloat16)
                a1[member, p, :, lanes] = a0[member, p, :, lanes] + (
                    TIME_STEP * rate[member]
                    + TIME_STEP * DIFFUSIVITY * laplace_at(0, half, p, lanes, member)
                )
            return carry

        lax.fori_loop(0, n_p, first_step, 0)
        if half == 0:
            first_sends(a1, 1)

    other_sends(a1, 1)
    line_ops(1)
    along_r(a1)
    lax.fori_loop(0, n_p, first_gradient, 0)

    for half in range(HALVES):
        lanes = pl.ds(half * LANES, LANES)
        wait_back(1, half)

        def last_step(p, carry):
            curl = curl_at(1, half, p, lanes)
            rate = cross(curl, [vel[member, p, :, lanes] for member in range(3)])
            low = [curl[member].astype(jnp.bfloat16).astype(jnp.float32) for member in range(3)]
            terms = cross([saved[1, member, p, :, lanes].astype(jnp.float32) for member in range(3)], low)
            for member in range(3):
                out[member, p, :, lanes] = (
                    0.5 * (a0[member, p, :, lanes] + a1[member, p, :, lanes])
                    + 0.5 * TIME_STEP * rate[member]
                    + 0.5 * TIME_STEP * DIFFUSIVITY * laplace_at(1, half, p, lanes, member)
                )
                vgrad[member, p, :, lanes] += 0.5 * TIME_STEP * terms[member]
            return carry

        lax.fori_loop(0, n_p, last_step, 0)
        for at, (held, there) in enumerate(((out, out_there), (vgrad, vgrad_there))):
            part = held.at[:, :, :, lanes]
            pltpu.make_async_copy(part, there.at[:, :, :, lanes], out_sem.at[at, half]).start()

    for sec in range(2):
        for half in range(HALVES):
            wait_bytes(qbuf.at[sec, half, :, :, pl.ds(0, 6 * n_q)], send_sem.at[0, sec, half])
            wait_bytes(pback.at[sec, half, pl.ds(0, 3), :, pl.ds(0, 14)], send_sem.at[1, sec, half])
            wait_bytes(pback.at[sec, half, pl.ds(0, 3)], send_sem.at[4, sec, half])
            wait_bytes(pback.at[sec, half, pl.ds(0, 3), :, pl.ds(0, 16)], send_sem.at[5, sec, half])
            wait_bytes(qres.at[sec, half, :, :, pl.ds(0, 3 * n_q)], send_sem.at[2, sec, half])
            wait_bytes(pback.at[sec, half, :, :, pl.ds(0, n_q - 2)], send_sem.at[3, sec, half])
            wait_bytes(mate.at[sec, :, :, :, pl.ds(half * LANES, LANES)], mate_send.at[sec, half])
            for at, held in enumerate((out, vgrad)):
                if sec == 0:
                    wait_bytes(held.at[:, :, :, pl.ds(half * LANES, LANES)], out_sem.at[at, half])


def solution(mesh):
    rows, cols = mesh.shape["row"], mesh.shape["col"]

    def local(adjoint_field, velocity, saved_field, gradient_in):
        _, n_p, n_q, length = adjoint_field.shape
        first, second = line_tables(length)
        by_zh = np.arange(length).reshape(4, 4, -1).transpose(1, 0, 2).reshape(4, -1)
        by_zl = np.arange(length).reshape(2, -1)

        def left_table(groups):
            return jnp.asarray(np.concatenate([first[groups], second[groups]], axis=1), jnp.float32)

        right = jnp.asarray(np.concatenate([first.T, second.T], axis=1), jnp.float32)
        field = jax.ShapeDtypeStruct(adjoint_field.shape, jnp.float32)
        q_lines = (2, HALVES, 3, 2, length, LANES)
        p_lines = (2, HALVES, 2, 3, 4, 4, length // 16, LANES)
        q_results = (2, HALVES, 5, 2, length // 2, LANES)
        p_results = (2, HALVES, 2, 5, 2, length // 4, LANES)
        back = (2, HALVES, 5, n_p, n_q, LANES)
        arrays = (
            adjoint_field, velocity, saved_field, gradient_in, left_table(by_zh), left_table(by_zl), right,
        )
        return pl.pallas_call(
            functools.partial(kernel, rows, cols),
            out_shape=(field, field),
            in_specs=[pl.BlockSpec(memory_space=pl.ANY)] * 7,
            out_specs=(pl.BlockSpec(memory_space=pl.ANY),) * 2,
            scratch_shapes=[
                pltpu.VMEM(field.shape, jnp.float32),
                pltpu.VMEM(field.shape, jnp.float32),
                pltpu.SemaphoreType.DMA((2, HALVES)),
                *(pltpu.VMEM(given.shape, given.dtype) for given in arrays),
                pltpu.SemaphoreType.DMA((HALVES + len(arrays) - 1,)),
                pltpu.VMEM((4, length // 2, 3 * length), jnp.bfloat16),
                pltpu.VMEM((2, length, 3 * length), jnp.bfloat16),
                pltpu.VMEM((3 * length, 2 * length), jnp.bfloat16),
                pltpu.VMEM(field.shape, jnp.float32),
                pltpu.VMEM((2, *field.shape), jnp.float32),
                pltpu.VMEM(field.shape, jnp.bfloat16),
                pltpu.VMEM((5, n_p, n_q, length), jnp.float32),
                pltpu.VMEM(q_lines, jnp.float32),
                pltpu.VMEM(p_lines, jnp.float32),
                pltpu.VMEM(q_results, jnp.float32),
                pltpu.VMEM(p_results, jnp.float32),
                pltpu.VMEM(back, jnp.float32),
                pltpu.VMEM(back, jnp.float32),
                pltpu.SemaphoreType.DMA((6, 2, HALVES)),
                pltpu.SemaphoreType.DMA((6, 2, HALVES)),
                pltpu.SemaphoreType.DMA((2, HALVES)),
                pltpu.SemaphoreType.DMA((2, HALVES, 4)),
            ],
            compiler_params=pltpu.CompilerParams(
                collective_id=0, has_side_effects=True, vmem_limit_bytes=60 * 2**20
            ),
        )(*arrays)

    placed = P(None, "col", "row", None)
    return jax.shard_map(
        local,
        mesh=mesh,
        in_specs=(placed, placed, P(None, None, "col", "row", None), placed),
        out_specs=(placed, placed),
        check_vma=False,
    )
```

profile of v0, /device:TPU:1, one launch (start us, length us, event | category | flops | bytes accessed | tf_op | source)
XLA Modules:
  0.0 121.4 jit_solution(9189240541716267314)
XLA Ops:
  0.6 117.7 %shard_map.86 = (f32[3,8,32,256]{3,2,1,0:T(8,128)}, f32[3,8,32,256]{3,2,1,0:T(8,128)}) custom-call(f32[3,8,32,256]{3,2,1,0:T(8,128)} %a0_in.1, f32[3,8,32,256]{3,2,1,0:T(8,128)} %vel_in.1, bf16[2,3,8,32,256]{4,3,2,1,0:T(8,128)(2,1)} %saved_in.1, f32[3,8,32,256]{3,2,1,0:T(8,128)} %grad_in.1, f32[4,128,256]{2,1,0:T(8,128)} %constant.7.clone.left_p_in, ...), custom_call_target="tpu_custom_call" | custom-call | tf_op jit(solution)/shard_map/pallas_call | solution.py:441
  118.4 0.0 copy-start
  118.4 2.2 %copy.11 = f32[3,8,32,256]{3,2,1,0:T(8,128)} copy(f32[3,8,32,256]{3,2,1,0:T(8,128)} %get-tuple-element.4) | data formatting | bytes 1572864
  120.5 0.0 copy-done
  120.5 0.9 copy.12
Async XLA Ops:
  118.4 2.2 %copy-start = (f32[3,8,32,256]{3,2,1,0:T(8,128)S(1)}, f32[3,8,32,256]{3,2,1,0:T(8,128)}, u32[]{:S(2)}) copy-start(f32[3,8,32,256]{3,2,1,0:T(8,128)} %get-tuple-element.5) | copy-start | bytes 2359300
where the time goes:
time: 122 us; the launch traced here: 121 us
  Pallas kernels  118 us (97%)
  local copies, waits for them, and re-layouts  3.04 us (2%)
    pallas_call x1, Pallas kernels, local(): pl.pallas_call(functools.partial(kernel, rows, cols), out_shape=(field, f...  118 us
    unnamed x4, local copies, waits for them, and re-layouts  3.04 us

commit v1 on v0

--- a/solution.py
+++ b/solution.py
@@ -43,7 +43,7 @@
     a0_in, vel_in, saved_in, grad_in, left_p_in, left_q_in, right_in,
     out_there, vgrad_there,
     out, vgrad, out_sem, a0, vel, saved, grad, left_p_f32, left_q_f32, right_f32, load_sem, left_p, left_q, right,
-    a1, mate, curl0, line_r, qbuf, pbuf, qres, pres, qback, pback, send_sem, recv_sem, mate_send, mate_recv,
+    a1, mate, curl0, line_r, qbuf, pbuf, qres, pres, qback, pback, send_sem, recv_sem, p_recv, mate_send, mate_recv,
 ):
     row, col = lax.axis_index("row"), lax.axis_index("col")
     n_p, n_q, length = a0.shape[1], a0.shape[2], a0.shape[3]
@@ -121,22 +121,24 @@
             pbuf.at[sec, half, role, :, lax.div(col, 8), zh, pl.ds(pl.multiple_of(lax.rem(col, 2) * n_p, n_p), n_p), :],
         )
 
+    def near_arrival(role, c):
+        return (1 - zl) * (5 + c) if role else zl * (1 + c)
+
     def send_line(field, sec, half, row_there, spot_there, zh_there, role, kind, arrival):
         src, dst = p_line(field, sec, half, row_there, spot_there, zh_there, role)
         pltpu.make_async_remote_copy(
-            src_ref=src, dst_ref=dst, send_sem=send_sem.at[kind, sec, half], recv_sem=recv_sem.at[arrival, sec, half],
+            src_ref=src, dst_ref=dst, send_sem=send_sem.at[kind, sec, half], recv_sem=p_recv.at[sec, half, arrival],
             device_id=(row_there, col_of(spot_there, zh_there)), device_id_type=MESH,
         ).start()
 
-    near_arrival = (1 + 3 * zl, 5 - 4 * zl)
-
-    def pass_on(sec, half):
+    def pass_on(sec, half, c):
+        y_from = lax.rem(lax.div(spot, 2) + 4 - c, 4)
         for role, source, there in ((0, below, above), (1, above, below)):
-            lines = pbuf.at[sec, half, role, :, :, source]
-            wait_bytes(lines, recv_sem.at[4 + role, sec, half])
+            lines = pbuf.at[sec, half, role, :, y_from, source]
+            wait_bytes(lines, p_recv.at[sec, half, 1 + 4 * role + c])
             pltpu.make_async_remote_copy(
-                src_ref=lines, dst_ref=pbuf.at[sec, half, 1 - role, :, :, source],
-                send_sem=send_sem.at[5, sec, half], recv_sem=recv_sem.at[1, sec, half],
+                src_ref=lines, dst_ref=pbuf.at[sec, half, 1 - role, :, y_from, source],
+                send_sem=send_sem.at[5, sec, half], recv_sem=p_recv.at[sec, half, 0],
                 device_id=(row, col_of(spot, there)), device_id_type=MESH,
             ).start()
 
@@ -177,24 +179,24 @@
         for core in range(2):
             there = y_there * 2 + core
             for role in range(2):
-                send_line(mate.at[sec], sec, half, mate_row, there, near, role, 4, near_arrival[role])
+                send_line(mate.at[sec], sec, half, mate_row, there, near, role, 4, near_arrival(role, c))
 
     def send_near(field, sec, half, c):
         y_there, _ = mate_part(c)
         for core in range(2):
             for role in range(2):
-                send_line(field, sec, half, row, y_there * 2 + core, near, role, 4, near_arrival[role])
+                send_line(field, sec, half, row, y_there * 2 + core, near, role, 4, near_arrival(role, c))
 
     def send_zh(field, sec, half):
         def to_spot(j, carry):
             for role in range(2):
-                send_line(field, sec, half, row, spot_at(j), zh, role, 1, 1)
+                send_line(field, sec, half, row, spot_at(j), zh, role, 1, 0)
             return carry
 
         lax.fori_loop(1, 8, to_spot, 0)
         for role in range(2):
             src, dst = p_line(field, sec, half, row, spot, zh, role)
-            here(src, dst, 1, sec, half)
+            pltpu.make_async_copy(src, dst, p_recv.at[sec, half, 0]).start()
 
     def parts(step):
         def body(c, carry):
@@ -214,15 +216,15 @@
         send_zh(field, sec, 1)
         send_q(field, sec, 1, row)
         send_q(mate.at[sec], sec, 0, mate_row)
-        parts(lambda c: pass_mate(sec, 1, c))
-        pass_on(sec, 0)
+        parts(lambda c: (pass_mate(sec, 1, c), pass_on(sec, 0, c)))
         send_q(mate.at[sec], sec, 1, mate_row)
-        pass_on(sec, 1)
 
     def line_ops(sec):
-        for half in range(HALVES):
-            p_ops(sec, half)
-            q_ops(sec, half)
+        q_ops(sec, 0)
+        parts(lambda c: pass_on(sec, 1, c))
+        p_ops(sec, 0)
+        p_ops(sec, 1)
+        q_ops(sec, 1)
 
     def stack(lines):
         high, low = split_parts(lines)
@@ -232,7 +234,7 @@
         return lines.reshape(length, LANES)
 
     def p_ops(sec, half):
-        wait_bytes(pbuf.at[sec, half, :, :, pl.ds(0, 3)], recv_sem.at[1, sec, half])
+        wait_bytes(pbuf.at[sec, half, :, :, pl.ds(0, 3)], p_recv.at[sec, half, 0])
         for role, beside in ((0, below), (1, above)):
             lines = jnp.concatenate([whole(pbuf[sec, half, role, 1]), whole(pbuf[sec, half, role, 2])], axis=1)
             table = jnp.concatenate([left_p[zh], left_p[beside]], axis=0)
@@ -463,7 +465,8 @@
                 pltpu.VMEM(back, jnp.float32),
                 pltpu.VMEM(back, jnp.float32),
                 pltpu.SemaphoreType.DMA((6, 2, HALVES)),
-                pltpu.SemaphoreType.DMA((6, 2, HALVES)),
+                pltpu.SemaphoreType.DMA((4, 2, HALVES)),
+                pltpu.SemaphoreType.DMA((2, HALVES, 9)),
                 pltpu.SemaphoreType.DMA((2, HALVES)),
                 pltpu.SemaphoreType.DMA((2, HALVES, 4)),
             ],

time: 122 us -> 120 us (0.984)
  Pallas kernels: 118 us -> 116 us
    pallas_call x1, Pallas kernels: 118 us -> 116 us  [local(): pl.pallas_call(functools.partial(kernel, rows, cols), out_shape=(field, f...]
where the time goes in v1:
time: 120 us
  Pallas kernels  116 us (97%)
  local copies, waits for them, and re-layouts  3.04 us (3%)
    pallas_call x1, Pallas kernels, local(): pl.pallas_call(functools.partial(kernel, rows, cols), out_shape=(field, f...  116 us
    unnamed x4, local copies, waits for them, and re-layouts  3.04 us

profile of v1, /device:TPU:1, one launch (start us, length us, event | category | flops | bytes accessed | tf_op | source)
XLA Modules:
  0.0 120.0 jit_solution(12572173425882242727)
XLA Ops:
  0.6 116.3 %shard_map.86 = (f32[3,8,32,256]{3,2,1,0:T(8,128)}, f32[3,8,32,256]{3,2,1,0:T(8,128)}) custom-call(f32[3,8,32,256]{3,2,1,0:T(8,128)} %a0_in.1, f32[3,8,32,256]{3,2,1,0:T(8,128)} %vel_in.1, bf16[2,3,8,32,256]{4,3,2,1,0:T(8,128)(2,1)} %saved_in.1, f32[3,8,32,256]{3,2,1,0:T(8,128)} %grad_in.1, f32[4,128,256]{2,1,0:T(8,128)} %constant.7.clone.left_p_in, ...), custom_call_target="tpu_custom_call" | custom-call | tf_op jit(solution)/shard_map/pallas_call | solution.py:443
  116.9 0.0 copy-start
  116.9 2.2 %copy.11 = f32[3,8,32,256]{3,2,1,0:T(8,128)} copy(f32[3,8,32,256]{3,2,1,0:T(8,128)} %get-tuple-element.4) | data formatting | bytes 1572864
  119.1 0.0 copy-done
  119.1 0.9 copy.12
Async XLA Ops:
  116.9 2.2 %copy-start = (f32[3,8,32,256]{3,2,1,0:T(8,128)S(1)}, f32[3,8,32,256]{3,2,1,0:T(8,128)}, u32[]{:S(2)}) copy-start(f32[3,8,32,256]{3,2,1,0:T(8,128)} %get-tuple-element.5) | copy-start | bytes 2359300
